TPU v7x, 32 devices: a whole 2x2x4 slice. The times are simulated.
32 devices in a mesh: dp: 4 (over z), expert: 8 (over y, x, core).
Axes of the slice: x: 2, y: 2, z: 4, core: 2. Of those that a mesh axis runs over, the one named last changes fastest.
Arguments:
- tokens: bfloat16 [1024, 7168], P('expert', 'dp'), may hold values from -6 to 6
- routes: int32 [1024, 4], P('expert'), may hold values from 0 to 7, all different within a row; in each aligned block of 128 rows (0 to 127, 128 to 255, ...) at most 96 rows name the same one
- gate_probs: float32 [1024, 4], P('expert'), may hold values from 0.05 to 0.5
- gate_up_weight: bfloat16 [8, 7168, 2, 1024], P('expert', 'dp'), may hold values from -0.0625 to 0.0625
- down_weight: bfloat16 [8, 1024, 7168], P('expert', None, 'dp'), may hold values from -0.1875 to 0.1875
- cotangent: bfloat16 [1024, 7168], P('expert', 'dp'), may hold values from -6 to 6
Outputs:
- mixed: bfloat16 [1024, 7168], P('expert', 'dp')
- token_grad: bfloat16 [1024, 7168], P('expert', 'dp')
- prob_grad: float32 [1024, 4], P('expert')
- gate_up_grad: bfloat16 [8, 7168, 2, 1024], P('expert', 'dp')
- down_grad: bfloat16 [8, 1024, 7168], P('expert', None, 'dp')
Inputs may be any that keep to these rules, and one draw needn't show every extreme that they name: `routes`: each row names 4 different experts. In each aligned block of 128 rows (the rows of one device) no expert is named by more than 96 rows, a bound that some block reaches.
All inputs are finite; a program needn't handle non-finite values.
Results may differ from a plain program's by a relative error of at most 0.0065.
Values may be sent and summed in bfloat16 or wider, within the bound.
No kernel may reach another device: no remote copies, remote signals or barrier semaphores. Data moves between devices by JAX's collectives and lax.ppermute only.
A program may use at most 128 MiB of HBM per device.

v0:
```python
import jax
import jax.numpy as jnp
from jax import lax
from jax.sharding import PartitionSpec as P


def silu_parts(pre_act):
    sigmoid_v = jax.nn.sigmoid(pre_act)
    return (pre_act * sigmoid_v, sigmoid_v * (1.0 + pre_act * (1.0 - sigmoid_v)))


def slot_table(route_block, experts, capacity):
    flat_routes = route_block.reshape(-1)
    onehot = (flat_routes[:, None] == jnp.arange(experts, dtype=jnp.int32)[None, :]).astype(
        jnp.int32
    )
    before = jnp.cumsum(onehot, axis=0) - onehot
    position = jnp.sum(before * onehot, axis=1)
    return flat_routes * capacity + position


def shards(tokens, routes, gate_probs, gate_up_weight, down_weight, cotangent):
    tok_rows, model_part = tokens.shape
    top_count = routes.shape[1]
    hidden = down_weight.shape[1]
    experts = lax.axis_size("expert")
    capacity = 3 * tok_rows * top_count // (2 * experts)
    slot_count = experts * capacity
    destination = slot_table(routes, experts, capacity)
    matches = jnp.arange(slot_count, dtype=jnp.int32)[:, None] == destination[None, :]
    picker = jnp.any(matches.reshape(slot_count, tok_rows, top_count), axis=2).astype(jnp.bfloat16)
    slot_weight = jnp.sum(jnp.where(matches, gate_probs.reshape(1, -1), 0.0), axis=1)
    token_send = jnp.dot(picker, tokens, preferred_element_type=jnp.float32).astype(jnp.bfloat16)
    token_send = token_send.reshape(experts, capacity, model_part)
    grad_send = (
        jnp.dot(picker, cotangent, preferred_element_type=jnp.float32) * slot_weight[:, None]
    ).astype(jnp.bfloat16)
    grad_send = grad_send.reshape(experts, capacity, model_part)
    joined = gate_up_weight.reshape(model_part, 2 * hidden)
    down_local = down_weight.reshape(hidden, model_part)
    token_recv = lax.all_to_all(token_send, "expert", split_axis=0, concat_axis=0, tiled=True)
    token_rows = token_recv.reshape(slot_count, model_part)
    pre_act = lax.psum(jnp.dot(token_rows, joined, preferred_element_type=jnp.float32), "dp")
    activated, slopes = silu_parts(pre_act[:, :hidden])
    hidden_act = (activated * pre_act[:, hidden:]).astype(jnp.bfloat16)
    expert_out = jnp.dot(hidden_act, down_local, preferred_element_type=jnp.float32).astype(
        jnp.bfloat16
    )
    out_send = expert_out.reshape(experts, capacity, model_part)
    out_back = lax.all_to_all(out_send, "expert", split_axis=0, concat_axis=0, tiled=True)
    grad_recv = lax.all_to_all(grad_send, "expert", split_axis=0, concat_axis=0, tiled=True)
    grad_rows = grad_recv.reshape(slot_count, model_part)
    down_grad = lax.dot_general(
        hidden_act, grad_rows, (((0,), (0,)), ((), ())), preferred_element_type=jnp.float32
    ).astype(jnp.bfloat16)
    partial_grad = lax.dot_general(
        grad_rows, down_local, (((1,), (1,)), ((), ())), preferred_element_type=jnp.float32
    )
    hidden_grad = lax.psum(partial_grad, "dp")
    act_grad = jnp.concatenate(
        [hidden_grad * pre_act[:, hidden:] * slopes, hidden_grad * activated], axis=1
    ).astype(jnp.bfloat16)
    gate_up_grad = lax.dot_general(
        token_rows, act_grad, (((0,), (0,)), ((), ())), preferred_element_type=jnp.float32
    ).astype(jnp.bfloat16)
    slot_grad = lax.dot_general(
        act_grad, joined, (((1,), (1,)), ((), ())), preferred_element_type=jnp.float32
    ).astype(jnp.bfloat16)
    grad_out_send = slot_grad.reshape(experts, capacity, model_part)
    grad_back = lax.all_to_all(grad_out_send, "expert", split_axis=0, concat_axis=0, tiled=True)
    returned = jnp.take(out_back.reshape(slot_count, model_part), destination, axis=0)
    returned = returned.reshape(tok_rows, top_count, model_part).astype(jnp.float32)
    returned_grad = jnp.take(grad_back.reshape(slot_count, model_part), destination, axis=0)
    returned_grad = returned_grad.reshape(tok_rows, top_count, model_part).astype(jnp.float32)
    mixed = jnp.sum(gate_probs[:, :, None] * returned, axis=1).astype(jnp.bfloat16)
    prob_part = jnp.sum(returned * cotangent.astype(jnp.float32)[:, None, :], axis=2)
    prob_grad = lax.psum(prob_part, "dp")
    token_grad = jnp.sum(returned_grad, axis=1).astype(jnp.bfloat16)
    return (
        mixed,
        token_grad,
        prob_grad,
        gate_up_grad.reshape(1, model_part, 2, hidden),
        down_grad.reshape(1, hidden, model_part),
    )


def solution(mesh):
    placed = (
        P("expert", "dp"),
        P("expert", None),
        P("expert", None),
        P("expert", "dp", None, None),
        P("expert", None, "dp"),
        P("expert", "dp"),
    )
    return jax.shard_map(
        shards,
        mesh=mesh,
        in_specs=placed,
        out_specs=(
            P("expert", "dp"),
            P("expert", "dp"),
            P("expert", None),
            P("expert", "dp", None, None),
            P("expert", None, "dp"),
        ),
        check_vma=False,
    )
```

profile of v0, /device:TPU:0, one launch (start us, length us, event | category | flops | bytes accessed | tf_op | source)
XLA Modules:
  0.0 578.2 jit_solution(15615102894399875981)
XLA Ops:
  7.2 0.8 copy.29
  8.0 0.1 eq.50
  8.1 0.1 eq.46
  8.3 1.1 reduce-window.6
  9.4 0.2 slice_reduce_fusion
  9.7 0.1 fusion.11
  9.8 0.1 reduce_sum.53
  9.9 0.8 copy.28
  10.7 0.1 broadcast_in_dim.29
  10.8 0.1 copy.31
  10.8 0.7 multiply_add_fusion.1
  11.5 0.2 fusion.9
  11.8 0.2 select_reduce_fusion
  12.0 3.4 multiply_convert_fusion
  15.4 5.2 all-to-all-start.2
  20.6 2.4 convolution_convert_fusion.3
  23.0 31.2 %all-to-all-done.2 = bf16[8,96,1792]{2,1,0:T(8,128)(2,1)S(1)} async-done(((bf16[8,96,1792]{2,1,0:T(8,128)(2,1)}), bf16[8,96,1792]{2,1,0:T(8,128)(2,1)S(1)}, u32[]{:S(2)}, u32[]{:S(2)}) %all-to-all-start.2) | async-done | bytes 2752544 | tf_op jit(solution)/shard_map/all_to_all | solution.py:51
  54.3 4.4 all-to-all-start
  58.7 0.2 all-reduce.3.cloned.1.call-start
  58.9 9.4 %copy.34 = bf16[224,8,2,1024]{3,1,2,0:T(8,128)(2,1)} copy(bf16[224,8,2,1024]{3,2,1,0:T(2,128)(2,1)} %bitcast.41) | data formatting | bytes 14680064
  68.3 4.7 fusion
  73.0 19.4 %all-to-all-done = bf16[8,96,1792]{2,1,0:T(8,128)(2,1)} async-done(((bf16[8,96,1792]{2,1,0:T(8,128)(2,1)}), bf16[8,96,1792]{2,1,0:T(8,128)(2,1)}, u32[]{:S(2)}, u32[]{:S(2)}) %all-to-all-start) | async-done | bytes 2752544 | tf_op jit(solution)/shard_map/all_to_all | solution.py:41
  92.4 10.6 %fusion.15 = f32[768,2048]{1,0:T(8,128)} fusion(bf16[768,1792]{1,0:T(8,128)(2,1)} %bitcast.3, bf16[1792,2048]{1,0:T(8,128)(2,1)} %bitcast.42), kind=kOutput, calls=%fused_computation.41 | convolution fusion | flops 5637144576 | bytes 16384000 | tf_op jit(solution)/shard_map/dot_general | solution.py:43
  102.9 0.0 all-reduce.3.cloned.1.call-update
  103.0 324.9 %all-reduce.3.cloned.1.call-done = (f32[768,2048]{1,0:T(8,128)}, f32[768,1024]{1,0:T(8,128)}) async-done(((f32[768,2048]{1,0:T(8,128)}, f32[768,1024]{1,0:T(8,128)}), (f32[768,2048]{1,0:T(8,128)}, f32[768,1024]{1,0:T(8,128)})) %all-reduce.3.cloned.1.call-update) | async-done | bytes 9437200 | tf_op jit(solution)/shard_map/psum | solution.py:43
  427.9 5.7 multiply_convert_fusion.2
  433.6 11.5 %convolution_convert_fusion.2 = bf16[768,1792]{1,0:T(8,128)(2,1)} fusion(bf16[1792,2048]{1,0:T(8,128)(2,1)} %bitcast.43, bf16[768,1024]{1,0:T(8,128)(2,1)S(1)} %get-tuple-element.26, bf16[768,1024]{1,0:T(8,128)(2,1)S(1)} %get-tuple-element.25), kind=kOutput, calls=%fused_computation.12 | convolution fusion | flops 5644812288 | bytes 13238272 | tf_op jit(solution)/shard_map/dot_general | solution.py:66
  445.1 4.0 all-to-all-start.3
  449.1 2.3 mul.82
  451.4 5.2 mul.83
  456.6 7.2 %fusion.4 = bf16[768,1792]{1,0:T(8,128)(2,1)} fusion(bf16[768,1024]{1,0:T(8,128)(2,1)} %get-tuple-element.27, bf16[1,1024,1792]{2,1,0:T(8,128)(2,1)} %param.12), kind=kOutput, calls=%fused_computation.11 | convolution fusion | flops 2819948544 | bytes 7995392 | tf_op jit(solution)/shard_map/dot_general | solution.py:46
  463.7 18.8 %all-to-all-done.3 = bf16[8,96,1792]{2,1,0:T(8,128)(2,1)S(1)} async-done(((bf16[8,96,1792]{2,1,0:T(8,128)(2,1)}), bf16[8,96,1792]{2,1,0:T(8,128)(2,1)S(1)}, u32[]{:S(2)}, u32[]{:S(2)}) %all-to-all-start.3) | async-done | bytes 2752544 | tf_op jit(solution)/shard_map/all_to_all | solution.py:70
  482.6 4.4 all-to-all-start.1
  487.0 10.3 %convolution_convert_fusion = bf16[1792,2048]{1,0:T(8,128)(2,1)} fusion(bf16[768,1792]{1,0:T(8,128)(2,1)} %bitcast.3, bf16[768,1024]{1,0:T(8,128)(2,1)} %copy-done.5, bf16[768,1024]{1,0:T(8,128)(2,1)} %copy-done.4), kind=kOutput, calls=%fused_computation.2 | convolution fusion | flops 5647106048 | bytes 13238272 | tf_op jit(solution)/shard_map/dot_general | solution.py:63
  497.3 12.8 %reshape.112 = bf16[1,1792,2,1024]{3,2,1,0:T(2,128)(2,1)} reshape(bf16[1792,2048]{1,0:T(8,128)(2,1)} %convolution_convert_fusion) | data formatting | bytes 14680064 | tf_op jit(solution)/shard_map/reshape | solution.py:83
  510.1 7.2 %fusion.7 = bf16[1,1024,1792]{2,1,0:T(8,128)(2,1)} fusion(bf16[768,1024]{1,0:T(8,128)(2,1)} %get-tuple-element.27, bf16[768,1792]{1,0:T(8,128)(2,1)} %bitcast.45), kind=kOutput, calls=%fused_computation.14 | convolution fusion | flops 2820407296 | bytes 7995392 | tf_op jit(solution)/shard_map/dot_general | solution.py:53
  517.2 3.1 gather_fusion.1
  520.4 0.3 all-to-all-done.1
  520.6 6.1 %gather_fusion = bf16[512,1792]{1,0:T(8,128)(2,1)S(1)} fusion(bf16[768,1792]{1,0:T(8,128)(2,1)} %bitcast.6, s32[1024]{0:T(1024)S(1)} %pad_clamp_fusion), kind=kCustom, calls=%fused_computation.clone | custom fusion | bytes 3672064 | tf_op jit(solution)/shard_map/jit(_take)/gather | solution.py:71
  526.7 4.4 broadcast_select_fusion
  531.1 5.1 reshape.114
  536.2 5.4 multiply_reduce_fusion.1
  541.6 4.2 reshape.111
  545.8 2.7 multiply_reduce_fusion
  548.4 0.1 reduce_sum.58
  548.6 17.6 %psum.23 = f32[128,4]{1,0:T(8,128)S(1)} all-reduce(f32[128,4]{1,0:T(8,128)S(1)} %reduce_sum.58), channel_id=1, replica_groups=mesh['dp'=4,'expert'=8] {'dp'}, use_global_device_ids=true, to_apply=%region_10.12 | all-reduce | flops 512 | bytes 4096 | tf_op jit(solution)/shard_map/psum | solution.py:77
  566.2 0.7 copy.33
  566.9 4.5 reduce_sum.56
  (20 shorter events, 0.1 us)
Async XLA Ops:
  7.2 13.4 %copy-start = (bf16[128,1792]{1,0:T(8,128)(2,1)S(1)}, bf16[128,1792]{1,0:T(8,128)(2,1)}, u32[]{:S(2)}) copy-start(bf16[128,1792]{1,0:T(8,128)(2,1)} %param.8) | copy-start | bytes 1376260
  15.4 38.8 %all-to-all-start.2 = ((bf16[8,96,1792]{2,1,0:T(8,128)(2,1)}), bf16[8,96,1792]{2,1,0:T(8,128)(2,1)S(1)}, u32[]{:S(2)}, u32[]{:S(2)}) async-start(bf16[8,96,1792]{2,1,0:T(8,128)(2,1)} %bitcast.7), calls=%async_computation.2 | async-start | bytes 5505024 | tf_op jit(solution)/shard_map/all_to_all | solution.py:51
  54.3 14.0 %copy-start.2 = (bf16[8,96,1792]{2,1,0:T(8,128)(2,1)}, bf16[8,96,1792]{2,1,0:T(8,128)(2,1)S(1)}, u32[]{:S(2)}) copy-start(bf16[8,96,1792]{2,1,0:T(8,128)(2,1)S(1)} %all-to-all-done.2) | copy-start | bytes 8257540
  54.3 38.1 %all-to-all-start = ((bf16[8,96,1792]{2,1,0:T(8,128)(2,1)}), bf16[8,96,1792]{2,1,0:T(8,128)(2,1)}, u32[]{:S(2)}, u32[]{:S(2)}) async-start(bf16[8,96,1792]{2,1,0:T(8,128)(2,1)} %bitcast.2), calls=%async_computation | async-start | bytes 5505024 | tf_op jit(solution)/shard_map/all_to_all | solution.py:41
  58.7 369.2 %all-reduce.3.cloned.1.call-start = ((), (), s32[]{:S(2)}) async-start(), calls=%async_computation.4 | async-start | bytes 18874368 | tf_op jit(solution)/shard_map/psum | solution.py:43
  58.9 9.4 %copy-start.6 = (bf16[1,1024,1792]{2,1,0:T(8,128)(2,1)S(1)}, bf16[1,1024,1792]{2,1,0:T(8,128)(2,1)}, u32[]{:S(2)}) copy-start(bf16[1,1024,1792]{2,1,0:T(8,128)(2,1)} %param.12) | copy-start | bytes 11010052
  433.6 11.5 %copy-start.4 = (bf16[768,1024]{1,0:T(8,128)(2,1)}, bf16[768,1024]{1,0:T(8,128)(2,1)S(1)}, u32[]{:S(2)}) copy-start(bf16[768,1024]{1,0:T(8,128)(2,1)S(1)} %get-tuple-element.25) | copy-start | bytes 4718596
  433.6 11.5 %copy-start.5 = (bf16[768,1024]{1,0:T(8,128)(2,1)}, bf16[768,1024]{1,0:T(8,128)(2,1)S(1)}, u32[]{:S(2)}) copy-start(bf16[768,1024]{1,0:T(8,128)(2,1)S(1)} %get-tuple-element.26) | copy-start | bytes 4718596
  445.1 4.0 copy-start.3
  445.1 37.5 %all-to-all-start.3 = ((bf16[8,96,1792]{2,1,0:T(8,128)(2,1)}), bf16[8,96,1792]{2,1,0:T(8,128)(2,1)S(1)}, u32[]{:S(2)}, u32[]{:S(2)}) async-start(bf16[8,96,1792]{2,1,0:T(8,128)(2,1)} %bitcast.47), calls=%async_computation.3 | async-start | bytes 5505024 | tf_op jit(solution)/shard_map/all_to_all | solution.py:70
  482.6 38.1 %all-to-all-start.1 = ((bf16[8,96,1792]{2,1,0:T(8,128)(2,1)}), bf16[8,96,1792]{2,1,0:T(8,128)(2,1)}, u32[]{:S(2)}, u32[]{:S(2)}) async-start(bf16[8,96,1792]{2,1,0:T(8,128)(2,1)} %bitcast.46), calls=%async_computation.1 | async-start | bytes 5505024 | tf_op jit(solution)/shard_map/all_to_all | solution.py:50
  541.6 29.7 %copy-start.1 = (bf16[128,1792]{1,0:T(8,128)(2,1)S(1)}, bf16[128,1792]{1,0:T(8,128)(2,1)}, u32[]{:S(2)}) copy-start(bf16[128,1792]{1,0:T(8,128)(2,1)} %param.8) | copy-start | bytes 1376260
Sparse Core Ops, SparseCore 0:
  103.1 324.7 all-reduce.2
where the time goes:
time: 579 us; the launch traced here: 578 us
  waiting for transfers between devices  395 us (68%)
  matrix products  57.2 us (10%)
  local copies, waits for them, and re-layouts  51.2 us (9%)
  other arithmetic  25.1 us (4%)
  starting transfers between devices  18.2 us (3%)
  blocking collectives  17.6 us (3%)
  between operations  14.2 us (2%)
    psum x1, waiting for transfers between devices, shards(): lax.psum(jnp.dot(token_rows, joined, preferred_element_type=jnp.float32),...  325 us
    all_to_all x1, waiting for transfers between devices, shards(): lax.all_to_all(grad_send, 'expert', split_axis=0, concat_axis=0, tiled=True)  31.2 us
    all_to_all x1, waiting for transfers between devices, shards(): lax.all_to_all(token_send, 'expert', split_axis=0, concat_axis=0, tiled=T...  19.4 us
    all_to_all x1, waiting for transfers between devices, shards(): lax.all_to_all(grad_out_send, 'expert', split_axis=0, concat_axis=0, tile...  18.8 us
    psum x1, blocking collectives, shards(): prob_grad = lax.psum(prob_part, 'dp')  17.6 us
    reshape x1, local copies, waits for them, and re-layouts, shards(): gate_up_grad.reshape(1, model_part, 2, hidden)  12.8 us
    unnamed x18, local copies, waits for them, and re-layouts  11.7 us
  transfers between devices with their start and end apart: 5, of which 5 were waited for; matrix products, arithmetic and copies ran while one was open for 11% of the time, Pallas kernels for 0%

commit v1 on v0

--- a/solution.py
+++ b/solution.py
@@ -74,7 +74,11 @@
     returned_grad = returned_grad.reshape(tok_rows, top_count, model_part).astype(jnp.float32)
     mixed = jnp.sum(gate_probs[:, :, None] * returned, axis=1).astype(jnp.bfloat16)
     prob_part = jnp.sum(returned * cotangent.astype(jnp.float32)[:, None, :], axis=2)
-    prob_grad = lax.psum(prob_part, "dp")
+    prob_grad = prob_part
+    for hop in (1, 2):
+        prob_grad = prob_grad + lax.ppermute(
+            prob_grad, "dp", [(dev, dev ^ hop) for dev in range(4)]
+        )
     token_grad = jnp.sum(returned_grad, axis=1).astype(jnp.bfloat16)
     return (
         mixed,

time: 579 us -> 556 us (0.960)
  blocking collectives: 17.6 us -> 0 us
    all_to_all x1, waiting for transfers between devices: 18.8 us -> 0.01 us  [shards(): lax.all_to_all(grad_out_send, 'expert', split_axis=0, concat_axis=0, tile...]
    psum x1 -> x0, blocking collectives: 17.6 us -> none  [shards(): prob_grad = lax.psum(prob_part, 'dp')]
    all_to_all x1, waiting for transfers between devices: 0.27 us -> 15.2 us  [shards(): lax.all_to_all(out_send, 'expert', split_axis=0, concat_axis=0, tiled=True)]
    unnamed x18 -> x22, local copies, waits for them, and re-layouts: 11.7 us -> 11.7 us
  transfers between devices with their start and end apart: 5 -> 7, of which waited for: 5 -> 4; matrix products, arithmetic and copies ran while one was open for 11% -> 18% of each run, Pallas kernels for 0% -> 0%
where the time goes in v1:
time: 556 us; the launch traced here: 555 us
  waiting for transfers between devices  391 us (70%)
  matrix products  53.8 us (10%)
  local copies, waits for them, and re-layouts  49.6 us (9%)
  other arithmetic  26.2 us (5%)
  starting transfers between devices  20.2 us (4%)
  between operations  14.2 us (3%)
    psum x1, waiting for transfers between devices, shards(): lax.psum(jnp.dot(token_rows, joined, preferred_element_type=jnp.float32),...  325 us
    all_to_all x1, waiting for transfers between devices, shards(): lax.all_to_all(grad_send, 'expert', split_axis=0, concat_axis=0, tiled=True)  31.2 us
    all_to_all x1, waiting for transfers between devices, shards(): lax.all_to_all(token_send, 'expert', split_axis=0, concat_axis=0, tiled=T...  19.4 us
    all_to_all x1, waiting for transfers between devices, shards(): lax.all_to_all(out_send, 'expert', split_axis=0, concat_axis=0, tiled=True)  15.2 us
    reshape x1, local copies, waits for them, and re-layouts, shards(): gate_up_grad.reshape(1, model_part, 2, hidden)  12.8 us
    unnamed x22, local copies, waits for them, and re-layouts  11.7 us
  transfers between devices with their start and end apart: 7, of which 4 were waited for; matrix products, arithmetic and copies ran while one was open for 18% of the time, Pallas kernels for 0%

profile of v1, /device:TPU:0, one launch (start us, length us, event | category | flops | bytes accessed | tf_op | source)
XLA Modules:
  0.0 554.8 jit_solution(8451957400823044883)
XLA Ops:
  7.2 0.8 copy.29
  8.0 0.1 eq.50
  8.1 0.1 eq.46
  8.3 1.1 reduce-window.6
  9.4 0.2 slice_reduce_fusion
  9.7 0.1 fusion.11
  9.8 0.1 reduce_sum.53
  9.9 0.8 copy.28
  10.7 0.1 broadcast_in_dim.29
  10.8 0.1 copy.31
  10.8 0.7 multiply_add_fusion.1
  11.5 0.2 fusion.9
  11.8 0.2 select_reduce_fusion
  12.0 3.4 multiply_convert_fusion
  15.4 5.2 all-to-all-start.2
  20.6 2.4 convolution_convert_fusion.3
  23.0 31.2 %all-to-all-done.2 = bf16[8,96,1792]{2,1,0:T(8,128)(2,1)S(1)} async-done(((bf16[8,96,1792]{2,1,0:T(8,128)(2,1)}), bf16[8,96,1792]{2,1,0:T(8,128)(2,1)S(1)}, u32[]{:S(2)}, u32[]{:S(2)}) %all-to-all-start.2) | async-done | bytes 2752544 | tf_op jit(solution)/shard_map/all_to_all | solution.py:51
  54.3 4.4 all-to-all-start
  58.7 0.2 all-reduce.3.cloned.1.call-start
  58.9 9.4 %copy.34 = bf16[224,8,2,1024]{3,1,2,0:T(8,128)(2,1)} copy(bf16[224,8,2,1024]{3,2,1,0:T(2,128)(2,1)} %bitcast.41) | data formatting | bytes 14680064
  68.3 4.7 fusion
  73.0 19.4 %all-to-all-done = bf16[8,96,1792]{2,1,0:T(8,128)(2,1)} async-done(((bf16[8,96,1792]{2,1,0:T(8,128)(2,1)}), bf16[8,96,1792]{2,1,0:T(8,128)(2,1)}, u32[]{:S(2)}, u32[]{:S(2)}) %all-to-all-start) | async-done | bytes 2752544 | tf_op jit(solution)/shard_map/all_to_all | solution.py:41
  92.4 10.7 %fusion.15 = f32[768,2048]{1,0:T(8,128)} fusion(bf16[768,1792]{1,0:T(8,128)(2,1)} %bitcast.3, bf16[1792,2048]{1,0:T(8,128)(2,1)} %bitcast.42), kind=kOutput, calls=%fused_computation.41 | convolution fusion | flops 5637144576 | bytes 16384000 | tf_op jit(solution)/shard_map/dot_general | solution.py:43
  103.1 0.0 all-reduce.3.cloned.1.call-update
  103.1 324.9 %all-reduce.3.cloned.1.call-done = (f32[768,2048]{1,0:T(8,128)}, f32[768,1024]{1,0:T(8,128)}) async-done(((f32[768,2048]{1,0:T(8,128)}, f32[768,1024]{1,0:T(8,128)}), (f32[768,2048]{1,0:T(8,128)}, f32[768,1024]{1,0:T(8,128)})) %all-reduce.3.cloned.1.call-update) | async-done | bytes 9437200 | tf_op jit(solution)/shard_map/psum | solution.py:43
  428.0 6.2 %multiply_convert_fusion.2 = (bf16[768,1024]{1,0:T(8,128)(2,1)}, bf16[768,1024]{1,0:T(8,128)(2,1)}, bf16[768,1024]{1,0:T(8,128)(2,1)S(1)}) fusion(f32[768,1024]{1,0:T(8,128)} %get-tuple-element.22, f32[768,2048]{1,0:T(8,128)} %get-tuple-element.21), kind=kLoop, calls=%fused_computation.17 | loop fusion | flops 11796480 | bytes 14155776 | tf_op jit(solution)/shard_map/convert.2
  434.2 4.4 fusion.4
  438.6 4.0 all-to-all-start.1
  442.6 2.3 mul.82
  444.9 5.2 mul.83
  450.1 10.8 %convolution_convert_fusion.2 = bf16[768,1792]{1,0:T(8,128)(2,1)} fusion(bf16[1792,2048]{1,0:T(8,128)(2,1)} %bitcast.43, bf16[768,1024]{1,0:T(8,128)(2,1)} %get-tuple-element.26, bf16[768,1024]{1,0:T(8,128)(2,1)} %get-tuple-element.25), kind=kOutput, calls=%fused_computation.12 | convolution fusion | flops 5644812288 | bytes 13238272 | tf_op jit(solution)/shard_map/dot_general | solution.py:66
  460.9 15.2 %all-to-all-done.1 = bf16[8,96,1792]{2,1,0:T(8,128)(2,1)S(1)} async-done(((bf16[8,96,1792]{2,1,0:T(8,128)(2,1)}), bf16[8,96,1792]{2,1,0:T(8,128)(2,1)S(1)}, u32[]{:S(2)}, u32[]{:S(2)}) %all-to-all-start.1) | async-done | bytes 2752544 | tf_op jit(solution)/shard_map/all_to_all | solution.py:50
  476.1 4.4 all-to-all-start.3
  480.5 10.3 %convolution_convert_fusion = bf16[1792,2048]{1,0:T(8,128)(2,1)} fusion(bf16[768,1792]{1,0:T(8,128)(2,1)} %bitcast.3, bf16[768,1024]{1,0:T(8,128)(2,1)} %get-tuple-element.26, bf16[768,1024]{1,0:T(8,128)(2,1)} %get-tuple-element.25), kind=kOutput, calls=%fused_computation.2 | convolution fusion | flops 5647106048 | bytes 13238272 | tf_op jit(solution)/shard_map/dot_general | solution.py:63
  490.8 12.8 %reshape.112 = bf16[1,1792,2,1024]{3,2,1,0:T(2,128)(2,1)} reshape(bf16[1792,2048]{1,0:T(8,128)(2,1)} %convolution_convert_fusion) | data formatting | bytes 14680064 | tf_op jit(solution)/shard_map/reshape | solution.py:87
  503.6 7.2 %fusion.7 = bf16[1,1024,1792]{2,1,0:T(8,128)(2,1)} fusion(bf16[768,1024]{1,0:T(8,128)(2,1)} %copy-done.6, bf16[768,1792]{1,0:T(8,128)(2,1)} %bitcast.45), kind=kOutput, calls=%fused_computation.14 | convolution fusion | flops 2820407296 | bytes 7995392 | tf_op jit(solution)/shard_map/dot_general | solution.py:53
  510.7 3.2 gather_fusion
  513.9 3.2 multiply_reduce_fusion
  517.1 0.1 reduce_sum.58
  517.3 0.1 collective-permute-start
  517.4 7.1 %gather_fusion.1 = bf16[512,1792]{1,0:T(8,128)(2,1)} fusion(bf16[768,1792]{1,0:T(8,128)(2,1)} %bitcast.10, s32[1024]{0:T(1024)S(1)} %pad_clamp_fusion), kind=kCustom, calls=%fused_computation.1.clone | custom fusion | bytes 3672064 | tf_op jit(solution)/shard_map/jit(_take)/gather | solution.py:73
  524.4 4.3 broadcast_select_fusion
  528.8 5.1 reshape.114
  533.9 1.9 collective-permute-start.1
  535.8 5.5 multiply_reduce_fusion.1
  541.3 1.5 reshape.111
  542.7 4.5 reduce_sum.56
  547.3 0.7 copy.33
  (29 shorter events, 0.1 us)
Async XLA Ops:
  7.2 13.4 %copy-start = (bf16[128,1792]{1,0:T(8,128)(2,1)S(1)}, bf16[128,1792]{1,0:T(8,128)(2,1)}, u32[]{:S(2)}) copy-start(bf16[128,1792]{1,0:T(8,128)(2,1)} %param.8) | copy-start | bytes 1376260
  15.4 38.8 %all-to-all-start.2 = ((bf16[8,96,1792]{2,1,0:T(8,128)(2,1)}), bf16[8,96,1792]{2,1,0:T(8,128)(2,1)S(1)}, u32[]{:S(2)}, u32[]{:S(2)}) async-start(bf16[8,96,1792]{2,1,0:T(8,128)(2,1)} %bitcast.7), calls=%async_computation.2 | async-start | bytes 5505024 | tf_op jit(solution)/shard_map/all_to_all | solution.py:51
  54.3 14.0 %copy-start.4 = (bf16[8,96,1792]{2,1,0:T(8,128)(2,1)}, bf16[8,96,1792]{2,1,0:T(8,128)(2,1)S(1)}, u32[]{:S(2)}) copy-start(bf16[8,96,1792]{2,1,0:T(8,128)(2,1)S(1)} %all-to-all-done.2) | copy-start | bytes 8257540
  54.3 38.1 %all-to-all-start = ((bf16[8,96,1792]{2,1,0:T(8,128)(2,1)}), bf16[8,96,1792]{2,1,0:T(8,128)(2,1)}, u32[]{:S(2)}, u32[]{:S(2)}) async-start(bf16[8,96,1792]{2,1,0:T(8,128)(2,1)} %bitcast.2), calls=%async_computation | async-start | bytes 5505024 | tf_op jit(solution)/shard_map/all_to_all | solution.py:41
  58.7 369.3 %all-reduce.3.cloned.1.call-start = ((), (), s32[]{:S(2)}) async-start(), calls=%async_computation.4 | async-start | bytes 18874368 | tf_op jit(solution)/shard_map/psum | solution.py:43
  58.9 9.4 %copy-start.7 = (bf16[1,1024,1792]{2,1,0:T(8,128)(2,1)S(1)}, bf16[1,1024,1792]{2,1,0:T(8,128)(2,1)}, u32[]{:S(2)}) copy-start(bf16[1,1024,1792]{2,1,0:T(8,128)(2,1)} %param.12) | copy-start | bytes 11010052
  428.0 6.2 %copy-start.8 = (bf16[1,1024,1792]{2,1,0:T(8,128)(2,1)S(1)}, bf16[1,1024,1792]{2,1,0:T(8,128)(2,1)}, u32[]{:S(2)}) copy-start(bf16[1,1024,1792]{2,1,0:T(8,128)(2,1)} %param.12) | copy-start | bytes 11010052
  434.2 4.4 copy-start.6
  438.6 4.0 copy-start.5
  438.6 37.5 %all-to-all-start.1 = ((bf16[8,96,1792]{2,1,0:T(8,128)(2,1)}), bf16[8,96,1792]{2,1,0:T(8,128)(2,1)S(1)}, u32[]{:S(2)}, u32[]{:S(2)}) async-start(bf16[8,96,1792]{2,1,0:T(8,128)(2,1)} %bitcast.47), calls=%async_computation.1 | async-start | bytes 5505024 | tf_op jit(solution)/shard_map/all_to_all | solution.py:50
  476.1 41.2 %all-to-all-start.3 = ((bf16[8,96,1792]{2,1,0:T(8,128)(2,1)}), bf16[8,96,1792]{2,1,0:T(8,128)(2,1)}, u32[]{:S(2)}, u32[]{:S(2)}) async-start(bf16[8,96,1792]{2,1,0:T(8,128)(2,1)} %bitcast.46), calls=%async_computation.3 | async-start | bytes 5505024 | tf_op jit(solution)/shard_map/all_to_all | solution.py:70
  517.3 16.6 %collective-permute-start = (f32[128,4]{1,0:T(8,128)S(1)}, f32[128,4]{1,0:T(8,128)S(1)}, u32[]{:S(2)}, u32[]{:S(2)}) collective-permute-start(f32[128,4]{1,0:T(8,128)S(1)} %reduce_sum.58), channel_id=1, source_target_pairs={{0,8},{8,0},{16,24},{24,16},{1,9},{9,1},{17,25},{25,17},{2,10},{10... | collective-permute-start | bytes 6152 | tf_op jit(solution)/shard_map/ppermute | solution.py:79
  517.3 7.1 %copy-start.2 = (bf16[512,1792]{1,0:T(8,128)(2,1)S(1)}, bf16[512,1792]{1,0:T(8,128)(2,1)}, u32[]{:S(2)}) copy-start(bf16[512,1792]{1,0:T(8,128)(2,1)} %gather_fusion) | copy-start | bytes 5505028
  533.9 7.4 %copy-start.3 = (bf16[512,1792]{1,0:T(8,128)(2,1)S(1)}, bf16[512,1792]{1,0:T(8,128)(2,1)}, u32[]{:S(2)}) copy-start(bf16[512,1792]{1,0:T(8,128)(2,1)} %get-tuple-element.28) | copy-start | bytes 5505028
  533.9 13.3 %collective-permute-start.1 = (f32[128,4]{1,0:T(8,128)S(1)}, f32[128,4]{1,0:T(8,128)S(1)}, u32[]{:S(2)}, u32[]{:S(2)}) collective-permute-start(f32[128,4]{1,0:T(8,128)S(1)} %add.36), channel_id=1, source_target_pairs={{0,16},{8,24},{16,0},{24,8},{1,17},{9,25},{17,1},{25,9},{2,18},{10... | collective-permute-start | bytes 6152 | tf_op jit(solution)/shard_map/ppermute | solution.py:79
  535.8 12.1 %copy-start.1 = (bf16[128,1792]{1,0:T(8,128)(2,1)S(1)}, bf16[128,1792]{1,0:T(8,128)(2,1)}, u32[]{:S(2)}) copy-start(bf16[128,1792]{1,0:T(8,128)(2,1)} %param.8) | copy-start | bytes 1376260
Sparse Core Ops, SparseCore 0:
  103.2 324.7 all-reduce.2
